TPU v7x, 128 devices: a whole 4x4x4 slice. The times are simulated.
128 devices in a mesh: dp: 4 (over y), expert: 16 (over z, x), tensor: 2 (over core).
Axes of the slice: x: 4, y: 4, z: 4, core: 2. Of those that a mesh axis runs over, the one named last changes fastest.
Arguments:
- tokens: bfloat16 [8192, 7168], P(('dp', 'expert')), parts along dimension 0, may hold values from -6 to 6
- route_expert: int32 [8192, 8], P(('dp', 'expert')), parts along dimension 0, may hold values from 0 to 15, all different within a row; in each aligned block of 128 rows (0 to 127, 128 to 255, ...) at most 72 rows name the same one
- route_weight: int32 [8192, 8], P(('dp', 'expert')), parts along dimension 0, may hold values from 1 to 4095
- gate_weight: bfloat16 [16, 7168, 1024], P('expert', None, 'tensor'), may hold values from -0.0625 to 0.0625
- up_weight: bfloat16 [16, 7168, 1024], P('expert', None, 'tensor'), may hold values from -0.0625 to 0.0625
- down_weight: bfloat16 [16, 1024, 7168], P('expert', 'tensor'), may hold values from -0.1875 to 0.1875
- gate_scale: float32 [16, 1024], P('expert', 'tensor'), may hold values from 0.5 to 2
- up_scale: float32 [16, 1024], P('expert', 'tensor'), may hold values from 0.5 to 2
- down_scale: float32 [16, 7168], P('expert'), may hold values from 0.5 to 2
Outputs:
- combined: bfloat16 [8192, 7168], P(('dp', 'expert'), 'tensor'), parts along dimension 0
There are 4 independent parts, one for each index of `dp`. A program takes and returns all parts, laid end to end along the dimension named above; an argument that names none is the same for every part. Nothing has to cross between parts.
Inputs may be any that keep to these rules, and one draw needn't show every extreme that they name: `route_expert`: within the 128 rows of one index of expert each expert is named at most 72 times, a bound that some block reaches; a token names 8 different experts.
All inputs are finite; a program needn't handle non-finite values.
Results may differ from a plain program's by a relative error of at most 0.0057.
Values may be sent and summed in bfloat16 or wider, within the bound.
A program may use at most 192 MiB of HBM per device.

v0:
```python
import jax
import jax.numpy as jnp
from jax import lax
from jax.sharding import PartitionSpec as P

ROUTE_SCALE = 2.5


def slot_numbers(route_block, experts):
    flat_ids = route_block.reshape(-1)
    one_hot = (flat_ids[:, None] == jnp.arange(experts, dtype=jnp.int32)[None, :]).astype(jnp.int32)
    earlier = jnp.cumsum(one_hot, axis=0) - one_hot
    return jnp.sum(earlier * one_hot, axis=1).reshape(route_block.shape)


def expert_math(blocks_in, w_gate, w_up, w_down, s_gate, s_up, s_down):
    gate_act = (
        jnp.einsum("slcd,ldf->slcf", blocks_in, w_gate, preferred_element_type=jnp.float32)
        * s_gate[None, :, None, :]
    )
    up_act = (
        jnp.einsum("slcd,ldf->slcf", blocks_in, w_up, preferred_element_type=jnp.float32)
        * s_up[None, :, None, :]
    )
    hidden = (jax.nn.silu(gate_act) * up_act).astype(jnp.bfloat16)
    return (
        jnp.einsum("slcf,lfd->slcd", hidden, w_down, preferred_element_type=jnp.float32)
        * s_down[None, :, None, :]
    )


def send_back(outputs_here):
    return lax.all_to_all(outputs_here, "expert", split_axis=0, concat_axis=0, tiled=True)


def body(
    tokens,
    route_expert,
    route_weight,
    gate_weight,
    up_weight,
    down_weight,
    gate_scale,
    up_scale,
    down_scale,
):
    tok_rows, model_width = tokens.shape
    top_count = route_expert.shape[1]
    groups = lax.axis_size("expert")
    cores = lax.axis_size("tensor")
    local_experts = gate_weight.shape[0]
    experts = local_experts * groups
    capacity = 9 * tok_rows * top_count // (8 * experts)
    half_width = model_width // cores
    slots = slot_numbers(route_expert, experts)
    target = route_expert * capacity + slots
    token_ids = jnp.repeat(jnp.arange(tok_rows, dtype=jnp.int32), top_count)
    table = (
        jnp.full((experts * capacity,), tok_rows, jnp.int32).at[target.reshape(-1)].set(token_ids)
    )
    padded = jnp.concatenate([tokens, jnp.zeros((1, model_width), jnp.bfloat16)], axis=0)
    send_rows = padded[table].reshape(experts, capacity, model_width)
    received = lax.all_to_all(send_rows, "expert", split_axis=0, concat_axis=0, tiled=True)
    row_count = received.shape[1]
    blocks_in = received.reshape(groups, local_experts, row_count, model_width)
    partial_value = expert_math(
        blocks_in, gate_weight, up_weight, down_weight, gate_scale, up_scale, down_scale
    )
    partial_value = partial_value.reshape(experts, row_count, model_width)
    reduced = lax.psum_scatter(partial_value, "tensor", scatter_dimension=2, tiled=True).astype(
        jnp.bfloat16
    )
    results = send_back(reduced)
    flat_out = results.reshape(experts * capacity, half_width)
    weights_f = route_weight.astype(jnp.float32)
    mix = ROUTE_SCALE * weights_f / jnp.sum(weights_f, axis=1, keepdims=True)
    combined = jnp.zeros((tok_rows, half_width), jnp.float32)
    for route_slot in range(top_count):
        combined = combined + mix[:, route_slot : route_slot + 1] * flat_out[
            target[:, route_slot]
        ].astype(jnp.float32)
    return combined.astype(jnp.bfloat16)


def solution(mesh):
    in_specs = (
        P(("dp", "expert"), None),
        P(("dp", "expert"), None),
        P(("dp", "expert"), None),
        P("expert", None, "tensor"),
        P("expert", None, "tensor"),
        P("expert", "tensor", None),
        P("expert", "tensor"),
        P("expert", "tensor"),
        P("expert", None),
    )
    out_specs = P(("dp", "expert"), "tensor")
    return jax.shard_map(body, mesh=mesh, in_specs=in_specs, out_specs=out_specs, check_vma=False)
```

profile of v0, /device:TPU:0, one launch (start us, length us, event | category | flops | bytes accessed | tf_op | source)
XLA Modules:
  0.0 521.3 jit_solution(11268874110472689230)
XLA Ops:
  6.5 0.0 reduce-scatter.2.cloned.1.call-start
  6.5 0.8 copy.24
  7.3 0.1 eq.29
  7.4 0.1 eq.25
  7.5 4.5 reduce-window.6
  12.0 0.1 slice.90
  12.1 0.1 copy.26
  12.3 0.1 copy.27
  12.4 0.1 broadcast_add_fusion
  12.5 0.1 reshape.94
  12.6 0.7 multiply_add_fusion
  13.3 0.1 copy.29
  13.4 0.1 reshape.95
  13.6 0.1 reshape.180
  13.7 4.3 scatter_custom_fusion
  18.0 1.7 concatenate.3
  19.7 13.5 %gather_fusion = bf16[1152,7168]{1,0:T(8,128)(2,1)} fusion(bf16[129,7168]{1,0:T(8,128)(2,1)S(1)} %concatenate.3, s32[2048]{0:T(1024)S(1)} %pad_clamp_fusion), kind=kCustom, calls=%fused_computation | custom fusion | bytes 33034752 | tf_op jit(solution)/shard_map/gather | solution.py:62
  33.2 191.3 %all_to_all.10 = bf16[16,72,7168]{2,1,0:T(8,128)(2,1)S(1)} all-to-all(bf16[16,72,7168]{2,1,0:T(8,128)(2,1)} %bitcast.123), channel_id=1, replica_groups=mesh['dp'=4,'expert'=16,'tensor'=2] {'expert'}, dimensions={0} | all-to-all | bytes 33030144 | tf_op jit(solution)/shard_map/all_to_all | solution.py:63
  224.5 0.0 copy-start.2
  224.5 0.0 copy-start.3
  224.5 13.4 %fusion.2 = f32[16,72,512]{2,1,0:T(8,128)S(1)} fusion(bf16[16,72,7168]{2,1,0:T(8,128)(2,1)S(1)} %all_to_all.10, bf16[1,7168,512]{2,1,0:T(8,128)(2,1)} %param.13), kind=kOutput, calls=%fused_computation.13 | convolution fusion | flops 8455716864 | bytes 26214400 | tf_op jit(solution)/shard_map/slcd,ldf->slcf/dot_general | solution.py:22
  237.9 0.0 copy-done.2
  237.9 0.0 copy-done.3
  237.9 0.0 copy-start.1
  237.9 12.7 %fusion.12 = bf16[16,72,512]{2,1,0:T(8,128)(2,1)S(1)} fusion(f32[16,72,512]{2,1,0:T(8,128)S(1)} %fusion.2, bf16[16,72,7168]{2,1,0:T(8,128)(2,1)S(1)} %all_to_all.10, bf16[1,7168,512]{2,1,0:T(8,128)(2,1)} %param.12, f32[512]{0:T(512)S(1)} %bitcast.128, f32[512]{0:T(512)S(1)} %bitcast.129), kind=kOutput, calls=%fused_computation.24 | convolution fusion | flops 8460435456 | bytes 27398144 | tf_op jit(solution)/shard_map/slcd,ldf->slcf/dot_general | solution.py:18
  250.6 0.0 copy-done.1
  250.6 17.1 %fusion = f32[16,72,7168]{2,1,0:T(8,128)} fusion(f32[7168]{0:T(1024)S(1)} %bitcast.127, bf16[16,72,512]{2,1,0:T(8,128)(2,1)S(1)} %fusion.12, bf16[1,512,7168]{2,1,0:T(8,128)(2,1)} %param.14), kind=kOutput, calls=%fused_computation.11 | convolution fusion | flops 8463974400 | bytes 41578496 | tf_op jit(solution)/shard_map/slcf,lfd->slcd/dot_general | solution.py:27
  267.7 0.0 reduce-scatter.2.cloned.1.call-update
  267.7 45.3 %reduce-scatter.2.cloned.1.call-done = f32[16,72,3584]{2,1,0:T(8,128)} async-done(((f32[16,72,7168]{2,1,0:T(8,128)}), f32[16,72,3584]{2,1,0:T(8,128)}) %reduce-scatter.2.cloned.1.call-update) | async-done | bytes 16515088 | tf_op jit(solution)/shard_map/reduce_scatter | solution.py:70
  313.0 8.8 %convert_element_type.47 = bf16[16,72,3584]{2,1,0:T(8,128)(2,1)} convert(f32[16,72,3584]{2,1,0:T(8,128)} %reduce-scatter.2.cloned.1.call-done) | non-fusion elementwise | flops 4128768 | bytes 24772608 | tf_op jit(solution)/shard_map/convert_element_type | solution.py:70
  321.8 0.0 copy-start
  321.8 7.4 %all-to-all-start.1 = ((bf16[16,72,3584]{2,1,0:T(8,128)(2,1)}), bf16[16,72,3584]{2,1,0:T(8,128)(2,1)}, u32[]{:S(2)}, u32[]{:S(2)}) async-start(bf16[16,72,3584]{2,1,0:T(8,128)(2,1)} %convert_element_type.47), calls=%async_computation.2 | async-start | bytes 16515072 | tf_op jit(solution)/shard_map/all_to_all | solution.py:33
  329.2 0.0 copy-done
  329.4 123.5 %all-to-all-done.1 = bf16[16,72,3584]{2,1,0:T(8,128)(2,1)} async-done(((bf16[16,72,3584]{2,1,0:T(8,128)(2,1)}), bf16[16,72,3584]{2,1,0:T(8,128)(2,1)}, u32[]{:S(2)}, u32[]{:S(2)}) %all-to-all-start.1) | async-done | bytes 8257568 | tf_op jit(solution)/shard_map/all_to_all | solution.py:33
  452.9 6.4 %gather_fusion.8 = bf16[128,3584]{1,0:T(8,128)(2,1)S(1)} fusion(bf16[1152,3584]{1,0:T(8,128)(2,1)} %bitcast.25, s32[1024]{0:T(1024)S(1)} %get-tuple-element.21), kind=kCustom, calls=%fused_computation.8 | custom fusion | bytes 1835520 | tf_op jit(solution)/shard_map/gather | solution.py:79
  459.3 6.4 %gather_fusion.7 = bf16[128,3584]{1,0:T(8,128)(2,1)S(1)} fusion(bf16[1152,3584]{1,0:T(8,128)(2,1)} %bitcast.25, s32[1024]{0:T(1024)S(1)} %get-tuple-element.22), kind=kCustom, calls=%fused_computation.7 | custom fusion | bytes 1835520 | tf_op jit(solution)/shard_map/gather | solution.py:79
  465.7 6.4 %gather_fusion.6 = bf16[128,3584]{1,0:T(8,128)(2,1)S(1)} fusion(bf16[1152,3584]{1,0:T(8,128)(2,1)} %bitcast.25, s32[1024]{0:T(1024)S(1)} %get-tuple-element.23), kind=kCustom, calls=%fused_computation.6 | custom fusion | bytes 1835520 | tf_op jit(solution)/shard_map/gather | solution.py:79
  472.2 7.4 %gather_fusion.5 = bf16[128,3584]{1,0:T(8,128)(2,1)} fusion(bf16[1152,3584]{1,0:T(8,128)(2,1)} %bitcast.25, s32[1024]{0:T(1024)S(1)} %get-tuple-element.24), kind=kCustom, calls=%fused_computation.5 | custom fusion | bytes 1835520 | tf_op jit(solution)/shard_map/gather | solution.py:79
  479.5 7.6 %gather_fusion.4 = bf16[128,3584]{1,0:T(8,128)(2,1)} fusion(bf16[1152,3584]{1,0:T(8,128)(2,1)} %bitcast.25, s32[1024]{0:T(1024)S(1)} %get-tuple-element.25), kind=kCustom, calls=%fused_computation.4 | custom fusion | bytes 1835520 | tf_op jit(solution)/shard_map/gather | solution.py:79
  487.2 7.4 %gather_fusion.3 = bf16[128,3584]{1,0:T(8,128)(2,1)} fusion(bf16[1152,3584]{1,0:T(8,128)(2,1)} %bitcast.25, s32[1024]{0:T(1024)S(1)} %get-tuple-element.26), kind=kCustom, calls=%fused_computation.3 | custom fusion | bytes 1835520 | tf_op jit(solution)/shard_map/gather | solution.py:79
  494.5 7.4 %gather_fusion.2 = bf16[128,3584]{1,0:T(8,128)(2,1)} fusion(bf16[1152,3584]{1,0:T(8,128)(2,1)} %bitcast.25, s32[1024]{0:T(1024)S(1)} %get-tuple-element.27), kind=kCustom, calls=%fused_computation.2 | custom fusion | bytes 1835520 | tf_op jit(solution)/shard_map/gather | solution.py:79
  501.9 7.4 %gather_fusion.1 = bf16[128,3584]{1,0:T(8,128)(2,1)} fusion(bf16[1152,3584]{1,0:T(8,128)(2,1)} %bitcast.25, s32[1024]{0:T(1024)S(1)} %get-tuple-element.28), kind=kCustom, calls=%fused_computation.1 | custom fusion | bytes 1835520 | tf_op jit(solution)/shard_map/gather | solution.py:79
  509.3 4.9 add_convert_fusion
  (17 shorter events, 0.2 us)
Async XLA Ops:
  6.5 306.5 %reduce-scatter.2.cloned.1.call-start = ((), (), s32[]{:S(2)}) async-start(), calls=%async_computation.3 | async-start | bytes 49545216 | tf_op jit(solution)/shard_map/reduce_scatter | solution.py:70
  224.5 13.4 %copy-start.2 = (f32[1,512]{1,0:T(1,128)S(1)}, f32[1,512]{1,0:T(1,128)}, u32[]{:S(2)}) copy-start(f32[1,512]{1,0:T(1,128)} %param.16) | copy-start | bytes 6148
  224.5 13.4 %copy-start.3 = (f32[1,512]{1,0:T(1,128)S(1)}, f32[1,512]{1,0:T(1,128)}, u32[]{:S(2)}) copy-start(f32[1,512]{1,0:T(1,128)} %param.15) | copy-start | bytes 6148
  237.9 12.7 %copy-start.1 = (f32[1,7168]{1,0:T(1,128)S(1)}, f32[1,7168]{1,0:T(1,128)}, u32[]{:S(2)}) copy-start(f32[1,7168]{1,0:T(1,128)} %param.17) | copy-start | bytes 86020
  321.8 7.4 %copy-start = (s32[128,8]{0,1:T(8,128)S(1)}, s32[128,8]{0,1:T(8,128)}, u32[]{:S(2)}) copy-start(s32[128,8]{0,1:T(8,128)} %param.11) | copy-start | bytes 12292
  321.8 131.0 %all-to-all-start.1 = ((bf16[16,72,3584]{2,1,0:T(8,128)(2,1)}), bf16[16,72,3584]{2,1,0:T(8,128)(2,1)}, u32[]{:S(2)}, u32[]{:S(2)}) async-start(bf16[16,72,3584]{2,1,0:T(8,128)(2,1)} %convert_element_type.47), calls=%async_computation.2 | async-start | bytes 16515072 | tf_op jit(solution)/shard_map/all_to_all | solution.py:33
Sparse Core Ops, SparseCore 0:
  267.9 45.1 reduce-scatter.1
where the time goes:
time: 526 us; the launch traced here: 521 us
  blocking collectives  191 us (36%)
  waiting for transfers between devices  169 us (32%)
  local copies, waits for them, and re-layouts  77.6 us (15%)
  matrix products  43.2 us (8%)
  other arithmetic  19.2 us (4%)
  between operations  13.8 us (3%)
  starting transfers between devices  7.43 us (1%)
    all_to_all x1, blocking collectives, body(): lax.all_to_all(send_rows, 'expert', split_axis=0, concat_axis=0, tiled=True)  191 us
    all_to_all x1, waiting for transfers between devices, send_back(): lax.all_to_all(outputs_here, 'expert', split_axis=0, concat_axis=0, tiled...  123 us
    gather x8, local copies, waits for them, and re-layouts, body(): flat_out[target[:, route_slot]].astype(jnp.float32)  56.4 us
    reduce_scatter x1, waiting for transfers between devices, body(): lax.psum_scatter(partial_value, 'tensor', scatter_dimension=2, tiled=True)  45.3 us
    dot_general x1, matrix products, expert_math(): jnp.einsum('slcf,lfd->slcd', hidden, w_down, preferred_element_type=jnp.f...  17.1 us
    gather x1, local copies, waits for them, and re-layouts, body(): send_rows = padded[table].reshape(experts, capacity, model_width)  13.5 us
    dot_general x1, matrix products, expert_math(): jnp.einsum('slcd,ldf->slcf', blocks_in, w_up, preferred_element_type=jnp....  13.4 us
    dot_general x1, matrix products, expert_math(): jnp.einsum('slcd,ldf->slcf', blocks_in, w_gate, preferred_element_type=jn...  12.7 us
  transfers between devices with their start and end apart: 2, of which 2 were waited for; matrix products, arithmetic and copies ran while one was open for 0% of the time, Pallas kernels for 0%

commit v1 on v0

v1 whole, which is shorter than its diff:
```python
import jax
import jax.numpy as jnp
from jax import lax
from jax.experimental import pallas as pl
from jax.experimental.pallas import tpu as pltpu
from jax.sharding import PartitionSpec as P

ROUTE_SCALE = 2.5
MESH = pl.DeviceIdType.MESH
SIDE = 4
TOK = 128
CAP = 72
PAIR = 2 * CAP
OFFSETS = (0, 1, 3, 2)
BF16 = jnp.bfloat16
F32 = jnp.float32


def kernel(
    tok_hbm,
    re_ref,
    rw_ref,
    wg_hbm,
    wu_hbm,
    wd_hbm,
    sg_ref,
    su_ref,
    sd_ref,
    out_hbm,
    x_buf,
    wg,
    wu,
    wd,
    tok,
    send,
    ret,
    hid,
    own,
    part_in,
    info,
    pick,
    mix_hi,
    mix_lo,
    loc_sem,
    tok_s,
    tok_r,
    info_s,
    info_r,
    x_s,
    x_r,
    sib_s,
    sib_r,
    hid_s,
    hid_r,
    y_s,
    y_r,
    part_s,
    part_r,
    wd_sem,
):
    half = tok.shape[2]
    ff = wg.shape[1]
    d = lax.axis_index("dp")
    e = lax.axis_index("expert")
    c = lax.axis_index("tensor")
    z, x = e // SIDE, e % SIDE
    odd = (z + x) % 2

    def spot(axis, off):
        along_x = odd if axis == 0 else 1 - odd
        nz = (z + (1 - along_x) * off) % SIDE
        nx = (x + along_x * off) % SIDE
        return nz * SIDE + nx

    def dev(axis, off):
        return (d, spot(axis, off), c)

    sibling = (d, e, 1 - c)
    mine = pl.ds(pl.multiple_of(c * half, 128), half)
    other = pl.ds(pl.multiple_of((1 - c) * half, 128), half)
    hid_mine = pl.ds(pl.multiple_of(c * ff, 128), ff)

    def remote(src, dst, ss, rs, to):
        return pltpu.make_async_remote_copy(
            src_ref=src, dst_ref=dst, send_sem=ss, recv_sem=rs, device_id=to, device_id_type=MESH
        )

    tok_load = pltpu.make_async_copy(tok_hbm.at[:, mine], tok.at[0, 0:TOK], loc_sem.at[0])
    wg_load = pltpu.make_async_copy(wg_hbm.at[0], wg, loc_sem.at[1])
    wu_load = pltpu.make_async_copy(wu_hbm.at[0], wu, loc_sem.at[2])
    wd_load = pltpu.make_async_copy(
        wd_hbm.at[0, :, mine], wd.at[hid_mine], loc_sem.at[3]
    )
    tok_load.start()

    peers = [dev(a, o) for a in (0, 1) for o in (1, 3, 2)] + [sibling]
    barrier = pltpu.get_barrier_semaphore()
    for to in peers:
        pl.semaphore_signal(barrier, inc=1, device_id=to, device_id_type=MESH)
    pl.semaphore_wait(barrier, len(peers))

    tok_dst = (tok.at[1, 0:TOK], tok.at[1, TOK : 2 * TOK], tok.at[0, TOK : 2 * TOK])
    tok_cp = [
        remote(tok_hbm.at[:, mine], tok_dst[i], tok_s.at[i], tok_r.at[i], dev(0, (1, 3, 2)[i]))
        for i in range(3)
    ]
    for cp in tok_cp:
        cp.start()
    wg_load.start()
    wu_load.start()
    wd_load.start()
    wd_cp = remote(
        wd_hbm.at[0, :, other], wd.at[hid_mine], wd_sem.at[0], wd_sem.at[1], sibling
    )
    wd_cp.start()

    lane = lax.broadcasted_iota(jnp.int32, (TOK, TOK), 1)
    row = lax.broadcasted_iota(jnp.int32, (TOK, TOK), 0)
    wf = rw_ref[...].astype(F32)
    mix = ROUTE_SCALE * wf / jnp.sum(wf, axis=1, keepdims=True)
    chosen = jnp.zeros((TOK, TOK), F32)
    weight = jnp.zeros((TOK, TOK), F32)
    for k in range(re_ref.shape[1]):
        hit = re_ref[:, k : k + 1] == lane
        chosen = chosen + jnp.where(hit, 1.0, 0.0)
        weight = weight + jnp.where(hit, mix[:, k : k + 1], 0.0)
    chosen_t = chosen.T
    weight_t = weight.T
    before = jnp.where(row < lane, 1.0, 0.0).astype(BF16)
    place_t = jnp.dot(chosen_t.astype(BF16), before, preferred_element_type=F32)
    place_t = jnp.where(chosen_t > 0.5, place_t, -1.0)
    info[0, 0:16] = place_t[0:16]
    info[0, 16:32] = weight_t[0:16]
    info_cp = [
        remote(
            info.at[0],
            info.at[(2, 3, 1)[i]],
            info_s.at[i],
            info_r.at[i],
            dev(0, (1, 3, 2)[i]),
        )
        for i in range(3)
    ]
    for cp in info_cp:
        cp.start()
    for cp in info_cp:
        cp.wait_recv()

    slot_iota = lax.broadcasted_iota(jnp.int32, (PAIR, 2 * TOK), 0).astype(F32)

    def rows_of(pair, q):
        ex = spot(1 - pair, OFFSETS[q])
        first = info[2 * pair, pl.ds(ex, 1), :]
        second = info[2 * pair + 1, pl.ds(ex, 1), :]
        second = jnp.where(second >= 0.0, second + float(CAP), -1.0)
        return jnp.concatenate([first, second], axis=1)

    for pair in range(2):
        for q in range(4):
            rows = rows_of(pair, q)
            sel = jnp.where(slot_iota == rows, 1.0, 0.0)
            pick[pair, q * PAIR : (q + 1) * PAIR] = sel.astype(BF16)

    tile = 256

    def gather(pair):
        self_rows = pl.ds((1 - pair) * PAIR, PAIR)

        def step(n, carry):
            cols = pl.ds(pl.multiple_of(n * tile, tile), tile)
            got = jnp.dot(pick[pair], tok[pair, :, cols], preferred_element_type=F32).astype(BF16)
            home = pl.ds(pl.multiple_of(c * half + n * tile, 128), tile)
            x_buf[0, self_rows, home] = got[0:PAIR]
            send[pair, :, cols] = got[PAIR:]
            return carry

        lax.fori_loop(0, half // tile, step, 0)

    def part_at(pair, q):
        return pair if q < 3 else 1 - pair

    x_cp = {}
    for pair in range(2):
        for q in range(1, 4):
            part = part_at(pair, q)
            x_cp[pair, q] = remote(
                send.at[pair, (q - 1) * PAIR : q * PAIR],
                x_buf.at[q, part * PAIR : (part + 1) * PAIR, mine],
                x_s.at[pair * 3 + q - 1],
                x_r.at[2 * (q - 1) + part],
                dev(1 - pair, OFFSETS[q]),
            )
    sib_cp = {}
    for s in range(4):
        for part in range(2):
            at = x_buf.at[s, part * PAIR : (part + 1) * PAIR, mine]
            sib_cp[s, part] = remote(
                at, at, sib_s.at[2 * s + part], sib_r.at[2 * s + part], sibling
            )

    tok_cp[0].wait_recv()
    tok_cp[1].wait_recv()
    gather(1)
    for q in (1, 2, 3):
        x_cp[1, q].start()
    sib_cp[0, 0].start()
    tok_load.wait()
    tok_cp[2].wait_recv()
    gather(0)
    for q in (1, 2, 3):
        x_cp[0, q].start()
    sib_cp[0, 1].start()

    for pair in range(2):
        blocks = []
        for q in range(4):
            rows = rows_of(pair, q)
            ex = spot(1 - pair, OFFSETS[q])
            w = jnp.concatenate(
                [
                    info[2 * pair, pl.ds(16 + ex, 1), :],
                    info[2 * pair + 1, pl.ds(16 + ex, 1), :],
                ],
                axis=1,
            )
            blocks.append(jnp.where(slot_iota == rows, w, 0.0))
        blocks.append(jnp.zeros((mix_hi.shape[2] - 4 * PAIR, 2 * TOK), F32))
        full = jnp.concatenate(blocks, axis=0).T
        hi = full.astype(BF16)
        mix_hi[pair] = hi
        mix_lo[pair] = (full - hi.astype(F32)).astype(BF16)

    wg_load.wait()
    wu_load.wait()

    y_cp = {}
    back = (0, 3, 1, 2)
    for s in range(1, 4):
        for part in range(2):
            to = dev(part, back[s])
            pair = part_at(part, s)
            y_cp[s, part] = remote(
                x_buf.at[s, part * PAIR : (part + 1) * PAIR, other],
                ret.at[pair, s * PAIR : (s + 1) * PAIR],
                y_s.at[2 * (s - 1) + part],
                y_r.at[pair * 3 + s - 1],
                to,
            )
    hid_tile = 256
    for s in range(4):
        if s > 0:
            for part in range(2):
                x_cp[part_at(part, s), s].wait_recv()
                sib_cp[s, part].start()
        for part in range(2):
            sib_cp[s, part].wait()
        slot = s % 2

        def gate_up(n, carry):
            cols = pl.ds(pl.multiple_of(n * hid_tile, hid_tile), hid_tile)
            rows = x_buf[s]
            g = jnp.dot(rows, wg[:, cols], preferred_element_type=F32) * sg_ref[0:1, cols]
            u = jnp.dot(rows, wu[:, cols], preferred_element_type=F32) * su_ref[0:1, cols]
            h = (g / (1.0 + jnp.exp(-g))) * u
            at = pl.ds(pl.multiple_of(c * ff + n * hid_tile, 128), hid_tile)
            hid[slot, :, at] = h.astype(BF16)
            return carry

        lax.fori_loop(0, ff // hid_tile, gate_up, 0)
        hid_cp = remote(
            hid.at[slot, :, hid_mine],
            hid.at[slot, :, hid_mine],
            hid_s.at[s],
            hid_r.at[s],
            sibling,
        )
        hid_cp.start()
        if s == 0:
            wd_load.wait()
            wd_cp.wait()
        hid_cp.wait()

        def down(n, carry):
            cols = pl.ds(pl.multiple_of(n * tile, tile), tile)
            scale_at = pl.ds(pl.multiple_of(c * half + n * tile, 128), tile)
            y = jnp.dot(hid[slot], wd[:, cols], preferred_element_type=F32)
            y = (y * sd_ref[0:1, scale_at]).astype(BF16)
            if s == 0:
                ret[1, 0:PAIR, cols] = y[0:PAIR]
                ret[0, 0:PAIR, cols] = y[PAIR:]
            else:
                at = pl.ds(pl.multiple_of((1 - c) * half + n * tile, 128), tile)
                x_buf[s, :, at] = y
            return carry

        lax.fori_loop(0, half // tile, down, 0)
        if s > 0:
            for part in range(2):
                y_cp[s, part].start()

    for cp in tok_cp + info_cp:
        cp.wait_send()

    def combine(pair):
        def step(n, carry):
            cols = pl.ds(pl.multiple_of(n * tile, tile), tile)
            rows = ret[pair, :, cols]
            k = rows.shape[0]
            total = jnp.dot(mix_hi[pair, :, 0:k], rows, preferred_element_type=F32)
            total = total + jnp.dot(mix_lo[pair, :, 0:k], rows, preferred_element_type=F32)
            if pair == 0:
                own[:, cols] = total[0:TOK]
                tok[0, TOK:, cols] = total[TOK:].astype(BF16)
            else:
                tok[1, :, cols] = total.astype(BF16)
            return carry

        lax.fori_loop(0, half // tile, step, 0)

    part_cp = [
        remote(tok.at[1, 0:TOK], part_in.at[0], part_s.at[0], part_r.at[0], dev(1, 3)),
        remote(tok.at[1, TOK : 2 * TOK], part_in.at[1], part_s.at[1], part_r.at[1], dev(1, 1)),
        remote(tok.at[0, TOK : 2 * TOK], part_in.at[2], part_s.at[2], part_r.at[2], dev(0, 2)),
    ]

    def wait_rows(pair):
        for q in range(1, 4):
            y_cp[q, part_at(pair, q)].wait_recv()

    wait_rows(1)
    combine(1)
    part_cp[0].start()
    part_cp[1].start()
    wait_rows(0)
    combine(0)
    part_cp[2].start()
    for cp in part_cp:
        cp.wait_recv()

    def finish(n, carry):
        cols = pl.ds(pl.multiple_of(n * tile, tile), tile)
        total = own[:, cols]
        for i in range(3):
            total = total + part_in[i, :, cols].astype(F32)
        tok[0, 0:TOK, cols] = total.astype(BF16)
        return carry

    lax.fori_loop(0, half // tile, finish, 0)
    store = pltpu.make_async_copy(tok.at[0, 0:TOK], out_hbm, loc_sem.at[4])
    store.start()
    for cp in list(x_cp.values()) + list(y_cp.values()) + part_cp:
        cp.wait_send()
    store.wait()


def body(
    tokens,
    route_expert,
    route_weight,
    gate_weight,
    up_weight,
    down_weight,
    gate_scale,
    up_scale,
    down_scale,
):
    rows, width = tokens.shape
    half = width // 2
    ff = gate_weight.shape[2]
    hbm = pl.BlockSpec(memory_space=pl.ANY)
    vmem = pl.BlockSpec(memory_space=pltpu.VMEM)
    dma = pltpu.SemaphoreType.DMA
    return pl.pallas_call(
        kernel,
        out_shape=jax.ShapeDtypeStruct((rows, half), BF16),
        in_specs=[hbm, vmem, vmem, hbm, hbm, hbm, vmem, vmem, vmem],
        out_specs=hbm,
        scratch_shapes=[
            pltpu.VMEM((4, 2 * PAIR, width), BF16),
            pltpu.VMEM((width, ff), BF16),
            pltpu.VMEM((width, ff), BF16),
            pltpu.VMEM((2 * ff, half), BF16),
            pltpu.VMEM((2, 2 * TOK, half), BF16),
            pltpu.VMEM((2, 3 * PAIR, half), BF16),
            pltpu.VMEM((2, 4 * PAIR, half), BF16),
            pltpu.VMEM((2, 2 * PAIR, 2 * ff), BF16),
            pltpu.VMEM((TOK, half), F32),
            pltpu.VMEM((3, TOK, half), BF16),
            pltpu.VMEM((4, 32, TOK), F32),
            pltpu.VMEM((2, 4 * PAIR, 2 * TOK), BF16),
            pltpu.VMEM((2, 2 * TOK, 640), BF16),
            pltpu.VMEM((2, 2 * TOK, 640), BF16),
            dma((5,)),
            dma((3,)),
            dma((3,)),
            dma((3,)),
            dma((3,)),
            dma((6,)),
            dma((6,)),
            dma((8,)),
            dma((8,)),
            dma((4,)),
            dma((4,)),
            dma((6,)),
            dma((6,)),
            dma((3,)),
            dma((3,)),
            dma((2,)),
        ],
        compiler_params=pltpu.CompilerParams(
            collective_id=0, has_side_effects=True, vmem_limit_bytes=63 * 2**20
        ),
        name="routed_ffn",
    )(
        tokens,
        route_expert,
        route_weight,
        gate_weight,
        up_weight,
        down_weight,
        gate_scale,
        up_scale,
        down_scale,
    )


def solution(mesh):
    in_specs = (
        P(("dp", "expert"), None),
        P(("dp", "expert"), None),
        P(("dp", "expert"), None),
        P("expert", None, "tensor"),
        P("expert", None, "tensor"),
        P("expert", "tensor", None),
        P("expert", "tensor"),
        P("expert", "tensor"),
        P("expert", None),
    )
    out_specs = P(("dp", "expert"), "tensor")
    return jax.shard_map(body, mesh=mesh, in_specs=in_specs, out_specs=out_specs, check_vma=False)
```

time: 526 us -> 230 us (0.44)
  Pallas kernels: 0 us -> 225 us
  blocking collectives: 191 us -> 0 us
  waiting for transfers between devices: 169 us -> 0 us
  local copies, waits for them, and re-layouts: 77.6 us -> 4.98 us
  matrix products: 43.2 us -> 0 us
  other arithmetic: 19.2 us -> 0 us
  between operations: 13.8 us -> 0.01 us
  starting transfers between devices: 7.43 us -> 0 us
    pallas_call x0 -> x1, Pallas kernels: none -> 225 us  [body(): pl.pallas_call(kernel, out_shape=jax.ShapeDtypeStruct((rows, half), BF16)...]
    all_to_all x1 -> x0, blocking collectives: 191 us -> none  [body(): lax.all_to_all(send_rows, 'expert', split_axis=0, concat_axis=0, tiled=True)]
    all_to_all x1 -> x0, waiting for transfers between devices: 123 us -> none  [send_back(): lax.all_to_all(outputs_here, 'expert', split_axis=0, concat_axis=0, tiled...]
    gather x9 -> x0, local copies, waits for them, and re-layouts: 69.9 us -> none  [the longest x8 56.4 us: body(): flat_out[target[:, route_slot]].astype(jnp.float32)]
    reduce_scatter x1 -> x0, waiting for transfers between devices: 45.3 us -> none  [body(): lax.psum_scatter(partial_value, 'tensor', scatter_dimension=2, tiled=True)]
    dot_general x3 -> x0, matrix products: 43.2 us -> none  [the longest x1 17.1 us: expert_math(): jnp.einsum('slcf,lfd->slcd', hidden, w_down, preferred_element_type=jnp.f...]
    convert_element_type x3 -> x0, other arithmetic: 13.7 us -> none  [the longest x1 8.77 us: body(): lax.psum_scatter(partial_value, 'tensor', scatter_dimension=2, tiled=True)]
    all_to_all x1 -> x0, starting transfers between devices: 7.42 us -> none  [send_back(): lax.all_to_all(outputs_here, 'expert', split_axis=0, concat_axis=0, tiled...]
  transfers between devices with their start and end apart: 2 -> 0, of which waited for: 2 -> 0; matrix products, arithmetic and copies ran while one was open for 0% -> 0% of each run, Pallas kernels for 0% -> 0%
where the time goes in v1:
time: 230 us
  Pallas kernels  225 us (98%)
  local copies, waits for them, and re-layouts  4.98 us (2%)
    pallas_call x1, Pallas kernels, body(): pl.pallas_call(kernel, out_shape=jax.ShapeDtypeStruct((rows, half), BF16)...  225 us
    unnamed x3, local copies, waits for them, and re-layouts  4.98 us

profile of v1, /device:TPU:0, one launch (start us, length us, event | category | flops | bytes accessed | tf_op | source)
XLA Modules:
  0.0 229.7 jit_solution(6492809910709134294)
XLA Ops:
  0.0 1.4 copy.10.re_ref
  1.4 1.4 copy.11.rw_ref
  2.8 224.8 %routed_ffn.1 = bf16[128,3584]{1,0:T(8,128)(2,1)} custom-call(bf16[128,7168]{1,0:T(8,128)(2,1)} %tok_hbm.1, s32[128,8]{1,0:T(8,128)} %copy.10.re_ref, s32[128,8]{1,0:T(8,128)} %copy.11.rw_ref, bf16[1,7168,512]{2,1,0:T(8,128)(2,1)} %wg_hbm.1, bf16[1,7168,512]{2,1,0:T(8,128)(2,1)} %wu_hbm.1, bf16[1,512,7168]{2,1,0:T(8,128)(2,1)} %wd_hbm.1, f32[1,512]{1,0:T(1,128)} %sg_ref.1, ...), custom_call_target="tpu_custom_call" | custom-call | tf_op jit(solution)/shard_map/routed_ffn/pallas_call | solution.py:373
  227.6 2.2 copy.13

commit v2 on v1

--- a/solution.py
+++ b/solution.py
@@ -37,6 +37,7 @@
     hid,
     own,
     part_in,
+    relay,
     info,
     pick,
     mix_hi,
@@ -56,6 +57,8 @@
     y_r,
     part_s,
     part_r,
+    relay_s,
+    relay_r,
     wd_sem,
 ):
     half = tok.shape[2]
@@ -99,13 +102,35 @@
         pl.semaphore_signal(barrier, inc=1, device_id=to, device_id_type=MESH)
     pl.semaphore_wait(barrier, len(peers))
 
-    tok_dst = (tok.at[1, 0:TOK], tok.at[1, TOK : 2 * TOK], tok.at[0, TOK : 2 * TOK])
-    tok_cp = [
-        remote(tok_hbm.at[:, mine], tok_dst[i], tok_s.at[i], tok_r.at[i], dev(0, (1, 3, 2)[i]))
-        for i in range(3)
-    ]
-    for cp in tok_cp:
-        cp.start()
+    chunk = half // 2
+    tile = 256
+    big = -(-chunk // (2 * tile)) * tile
+    ends = (0, big, chunk, 2 * chunk - big, half)
+    quarter = [pl.ds(ends[q], ends[q + 1] - ends[q]) for q in range(4)]
+    chunks = [pl.ds(k * chunk, chunk) for k in range(2)]
+
+    tok_cp = {}
+    for i, off in enumerate((1, 3)):
+        for q in range(4):
+            tok_cp[i, q] = remote(
+                tok_hbm.at[:, pl.ds(pl.multiple_of(c * half + ends[q], 128), ends[q + 1] - ends[q])],
+                tok.at[1, i * TOK : (i + 1) * TOK, quarter[q]],
+                tok_s.at[4 * i + q],
+                tok_r.at[4 * i + q],
+                dev(0, off),
+            )
+    for q in range(4):
+        tok_cp[0, q].start()
+        tok_cp[1, q ^ 1].start()
+    for q in range(4):
+        side = q % 2
+        tok_cp[2, q] = remote(
+            tok.at[1, side * TOK : (side + 1) * TOK, quarter[q]],
+            tok.at[0, TOK : 2 * TOK, quarter[q]],
+            tok_s.at[8 + q],
+            tok_r.at[8 + q],
+            dev(1, (1, 3)[side]),
+        )
     wg_load.start()
     wu_load.start()
     wd_load.start()
@@ -161,9 +186,7 @@
             sel = jnp.where(slot_iota == rows, 1.0, 0.0)
             pick[pair, q * PAIR : (q + 1) * PAIR] = sel.astype(BF16)
 
-    tile = 256
-
-    def gather(pair):
+    def gather(pair, k):
         self_rows = pl.ds((1 - pair) * PAIR, PAIR)
 
         def step(n, carry):
@@ -174,7 +197,7 @@
             send[pair, :, cols] = got[PAIR:]
             return carry
 
-        lax.fori_loop(0, half // tile, step, 0)
+        lax.fori_loop(k * chunk // tile, (k + 1) * chunk // tile, step, 0)
 
     def part_at(pair, q):
         return pair if q < 3 else 1 - pair
@@ -183,13 +206,15 @@
     for pair in range(2):
         for q in range(1, 4):
             part = part_at(pair, q)
-            x_cp[pair, q] = remote(
-                send.at[pair, (q - 1) * PAIR : q * PAIR],
-                x_buf.at[q, part * PAIR : (part + 1) * PAIR, mine],
-                x_s.at[pair * 3 + q - 1],
-                x_r.at[2 * (q - 1) + part],
-                dev(1 - pair, OFFSETS[q]),
-            )
+            for k in range(2):
+                home = pl.ds(pl.multiple_of(c * half + k * chunk, 128), chunk)
+                x_cp[pair, q, k] = remote(
+                    send.at[pair, (q - 1) * PAIR : q * PAIR, chunks[k]],
+                    x_buf.at[q, part * PAIR : (part + 1) * PAIR, home],
+                    x_s.at[2 * (pair * 3 + q - 1) + k],
+                    x_r.at[2 * (2 * (q - 1) + part) + k],
+                    dev(1 - pair, OFFSETS[q]),
+                )
     sib_cp = {}
     for s in range(4):
         for part in range(2):
@@ -198,18 +223,28 @@
                 at, at, sib_s.at[2 * s + part], sib_r.at[2 * s + part], sibling
             )
 
-    tok_cp[0].wait_recv()
-    tok_cp[1].wait_recv()
-    gather(1)
-    for q in (1, 2, 3):
-        x_cp[1, q].start()
-    sib_cp[0, 0].start()
-    tok_load.wait()
-    tok_cp[2].wait_recv()
-    gather(0)
-    for q in (1, 2, 3):
-        x_cp[0, q].start()
+    for k in range(2):
+        for side in range(2):
+            tok_cp[side, 2 * k + side].wait_recv()
+            tok_cp[2, 2 * k + side].start()
+        for side in range(2):
+            tok_cp[side, 2 * k + 1 - side].wait_recv()
+        gather(1, k)
+        for q in (1, 2):
+            x_cp[1, q, k].start()
+        if k == 0:
+            tok_load.wait()
+        else:
+            sib_cp[0, 0].start()
+        tok_cp[2, 2 * k].wait_recv()
+        tok_cp[2, 2 * k + 1].wait_recv()
+        gather(0, k)
+        for q in (1, 2):
+            x_cp[0, q, k].start()
     sib_cp[0, 1].start()
+    for k in range(2):
+        for pair in range(2):
+            x_cp[pair, 3, k].start()
 
     for pair in range(2):
         blocks = []
@@ -237,20 +272,22 @@
     back = (0, 3, 1, 2)
     for s in range(1, 4):
         for part in range(2):
-            to = dev(part, back[s])
             pair = part_at(part, s)
-            y_cp[s, part] = remote(
-                x_buf.at[s, part * PAIR : (part + 1) * PAIR, other],
-                ret.at[pair, s * PAIR : (s + 1) * PAIR],
-                y_s.at[2 * (s - 1) + part],
-                y_r.at[pair * 3 + s - 1],
-                to,
-            )
+            for k in range(2):
+                away = pl.ds(pl.multiple_of((1 - c) * half + k * chunk, 128), chunk)
+                y_cp[s, part, k] = remote(
+                    x_buf.at[s, part * PAIR : (part + 1) * PAIR, away],
+                    ret.at[pair, s * PAIR : (s + 1) * PAIR, chunks[k]],
+                    y_s.at[2 * (2 * (s - 1) + part) + k],
+                    y_r.at[2 * (pair * 3 + s - 1) + k],
+                    dev(part, back[s]),
+                )
     hid_tile = 256
     for s in range(4):
         if s > 0:
             for part in range(2):
-                x_cp[part_at(part, s), s].wait_recv()
+                for k in range(2):
+                    x_cp[part_at(part, s), s, k].wait_recv()
                 sib_cp[s, part].start()
         for part in range(2):
             sib_cp[s, part].wait()
@@ -293,64 +330,97 @@
                 x_buf[s, :, at] = y
             return carry
 
-        lax.fori_loop(0, half // tile, down, 0)
-        if s > 0:
-            for part in range(2):
-                y_cp[s, part].start()
-
-    for cp in tok_cp + info_cp:
+        for k in range(2):
+            lax.fori_loop(k * chunk // tile, (k + 1) * chunk // tile, down, 0)
+            if s > 0:
+                for part in range(2):
+                    y_cp[s, part, k].start()
+
+    for cp in list(tok_cp.values()) + info_cp:
         cp.wait_send()
 
-    def combine(pair):
+    def combine(pair, q):
         def step(n, carry):
             cols = pl.ds(pl.multiple_of(n * tile, tile), tile)
             rows = ret[pair, :, cols]
-            k = rows.shape[0]
-            total = jnp.dot(mix_hi[pair, :, 0:k], rows, preferred_element_type=F32)
-            total = total + jnp.dot(mix_lo[pair, :, 0:k], rows, preferred_element_type=F32)
+            depth = rows.shape[0]
+            total = jnp.dot(mix_hi[pair, :, 0:depth], rows, preferred_element_type=F32)
+            total = total + jnp.dot(mix_lo[pair, :, 0:depth], rows, preferred_element_type=F32)
+            first, second = total[0:TOK], total[TOK:]
             if pair == 0:
-                own[:, cols] = total[0:TOK]
-                tok[0, TOK:, cols] = total[TOK:].astype(BF16)
+                own[:, cols] = first
+                tok[0, TOK:, cols] = second.astype(BF16)
             else:
-                tok[1, :, cols] = total.astype(BF16)
+                passed = relay[:, cols].astype(F32)
+                if q % 2 == 0:
+                    second = second + passed
+                else:
+                    first = first + passed
+                tok[1, 0:TOK, cols] = first.astype(BF16)
+                tok[1, TOK:, cols] = second.astype(BF16)
             return carry
 
-        lax.fori_loop(0, half // tile, step, 0)
-
-    part_cp = [
-        remote(tok.at[1, 0:TOK], part_in.at[0], part_s.at[0], part_r.at[0], dev(1, 3)),
-        remote(tok.at[1, TOK : 2 * TOK], part_in.at[1], part_s.at[1], part_r.at[1], dev(1, 1)),
-        remote(tok.at[0, TOK : 2 * TOK], part_in.at[2], part_s.at[2], part_r.at[2], dev(0, 2)),
+        lax.fori_loop(ends[q] // tile, ends[q + 1] // tile, step, 0)
+
+    relay_cp = [
+        remote(
+            tok.at[0, TOK : 2 * TOK, quarter[q]],
+            relay.at[:, quarter[q]],
+            relay_s.at[q],
+            relay_r.at[q],
+            dev(0, (1, 3)[q % 2]),
+        )
+        for q in range(4)
     ]
-
-    def wait_rows(pair):
+    part_cp = {}
+    for i in range(2):
+        for k in range(2):
+            part_cp[i, k] = remote(
+                tok.at[1, i * TOK : (i + 1) * TOK, chunks[k]],
+                part_in.at[i, :, chunks[k]],
+                part_s.at[2 * i + k],
+                part_r.at[2 * i + k],
+                dev(1, (3, 1)[i]),
+            )
+
+    def wait_rows(pair, k):
         for q in range(1, 4):
-            y_cp[q, part_at(pair, q)].wait_recv()
-
-    wait_rows(1)
-    combine(1)
-    part_cp[0].start()
-    part_cp[1].start()
-    wait_rows(0)
-    combine(0)
-    part_cp[2].start()
-    for cp in part_cp:
-        cp.wait_recv()
+            y_cp[q, part_at(pair, q), k].wait_recv()
+
+    for k in range(2):
+        wait_rows(0, k)
+        for q in (2 * k, 2 * k + 1):
+            combine(0, q)
+            relay_cp[q].start()
+        wait_rows(1, k)
+        for q in (2 * k, 2 * k + 1):
+            relay_cp[q].wait_recv()
+            combine(1, q)
+        for i in range(2):
+            part_cp[i, k].start()
 
     def finish(n, carry):
         cols = pl.ds(pl.multiple_of(n * tile, tile), tile)
         total = own[:, cols]
-        for i in range(3):
+        for i in range(2):
             total = total + part_in[i, :, cols].astype(F32)
         tok[0, 0:TOK, cols] = total.astype(BF16)
         return carry
 
-    lax.fori_loop(0, half // tile, finish, 0)
-    store = pltpu.make_async_copy(tok.at[0, 0:TOK], out_hbm, loc_sem.at[4])
-    store.start()
-    for cp in list(x_cp.values()) + list(y_cp.values()) + part_cp:
+    stores = []
+    for k in range(2):
+        for i in range(2):
+            part_cp[i, k].wait_recv()
+        lax.fori_loop(k * chunk // tile, (k + 1) * chunk // tile, finish, 0)
+        store = pltpu.make_async_copy(
+            tok.at[0, 0:TOK, chunks[k]], out_hbm.at[:, chunks[k]], loc_sem.at[4 + k]
+        )
+        store.start()
+        stores.append(store)
+    for cp in [*x_cp.values(), *y_cp.values(), *part_cp.values(), *relay_cp]:
         cp.wait_send()
-    store.wait()
+    for store in stores:
+        store.wait()
 
 
 def body(
@@ -385,26 +455,29 @@
             pltpu.VMEM((2, 4 * PAIR, half), BF16),
             pltpu.VMEM((2, 2 * PAIR, 2 * ff), BF16),
             pltpu.VMEM((TOK, half), F32),
-            pltpu.VMEM((3, TOK, half), BF16),
+            pltpu.VMEM((2, TOK, half), BF16),
+            pltpu.VMEM((TOK, half), BF16),
             pltpu.VMEM((4, 32, TOK), F32),
             pltpu.VMEM((2, 4 * PAIR, 2 * TOK), BF16),
             pltpu.VMEM((2, 2 * TOK, 640), BF16),
             pltpu.VMEM((2, 2 * TOK, 640), BF16),
-            dma((5,)),
+            dma((6,)),
+            dma((12,)),
+            dma((12,)),
             dma((3,)),
             dma((3,)),
-            dma((3,)),
-            dma((3,)),
-            dma((6,)),
-            dma((6,)),
+            dma((12,)),
+            dma((12,)),
             dma((8,)),
             dma((8,)),
             dma((4,)),
             dma((4,)),
-            dma((6,)),
-            dma((6,)),
-            dma((3,)),
-            dma((3,)),
+            dma((12,)),
+            dma((12,)),
+            dma((4,)),
+            dma((4,)),
+            dma((4,)),
+            dma((4,)),
             dma((2,)),
         ],
         compiler_params=pltpu.CompilerParams(

time: 230 us -> 201 us (0.87)
  Pallas kernels: 225 us -> 195 us
    pallas_call x1, Pallas kernels: 225 us -> 195 us  [body(): pl.pallas_call(kernel, out_shape=jax.ShapeDtypeStruct((rows, half), BF16)...]
where the time goes in v2:
time: 201 us; the launch traced here: 200 us
  Pallas kernels  195 us (97%)
  local copies, waits for them, and re-layouts  4.98 us (2%)
    pallas_call x1, Pallas kernels, body(): pl.pallas_call(kernel, out_shape=jax.ShapeDtypeStruct((rows, half), BF16)...  195 us
    unnamed x3, local copies, waits for them, and re-layouts  4.98 us

profile of v2, /device:TPU:0, one launch (start us, length us, event | category | flops | bytes accessed | tf_op | source)
XLA Modules:
  0.0 200.5 jit_solution(17986192419893179684)
XLA Ops:
  0.0 1.4 copy.10.re_ref
  1.4 1.4 copy.11.rw_ref
  2.8 195.5 %routed_ffn.1 = bf16[128,3584]{1,0:T(8,128)(2,1)} custom-call(bf16[128,7168]{1,0:T(8,128)(2,1)} %tok_hbm.1, s32[128,8]{1,0:T(8,128)} %copy.10.re_ref, s32[128,8]{1,0:T(8,128)} %copy.11.rw_ref, bf16[1,7168,512]{2,1,0:T(8,128)(2,1)} %wg_hbm.1, bf16[1,7168,512]{2,1,0:T(8,128)(2,1)} %wu_hbm.1, bf16[1,512,7168]{2,1,0:T(8,128)(2,1)} %wd_hbm.1, f32[1,512]{1,0:T(1,128)} %sg_ref.1, ...), custom_call_target="tpu_custom_call" | custom-call | tf_op jit(solution)/shard_map/routed_ffn/pallas_call | solution.py:443
  198.3 2.2 %copy.13 = bf16[128,3584]{1,0:T(8,128)(2,1)} copy(bf16[128,3584]{1,0:T(8,128)(2,1)} %routed_ffn.1) | data formatting | bytes 1835008

commit v3 on v2

--- a/solution.py
+++ b/solution.py
@@ -119,9 +119,16 @@
                 tok_r.at[4 * i + q],
                 dev(0, off),
             )
-    for q in range(4):
-        tok_cp[0, q].start()
-        tok_cp[1, q ^ 1].start()
+
+    def next_quarter(q):
+        if q > 0:
+            tok_cp[0, q - 1].wait_send()
+            tok_cp[1, (q - 1) ^ 1].wait_send()
+        if q < 4:
+            tok_cp[0, q].start()
+            tok_cp[1, q ^ 1].start()
+
+    next_quarter(0)
     for q in range(4):
         side = q % 2
         tok_cp[2, q] = remote(
@@ -224,27 +231,29 @@
             )
 
     for k in range(2):
+        next_quarter(2 * k + 1)
         for side in range(2):
             tok_cp[side, 2 * k + side].wait_recv()
             tok_cp[2, 2 * k + side].start()
+        next_quarter(2 * k + 2)
         for side in range(2):
             tok_cp[side, 2 * k + 1 - side].wait_recv()
+        if k == 1:
+            for q in (1, 2):
+                x_cp[1, q, 0].start()
         gather(1, k)
-        for q in (1, 2):
-            x_cp[1, q, k].start()
-        if k == 0:
+        if k == 1:
+            sib_cp[0, 0].start()
+            for q in (1, 2):
+                x_cp[1, q, 1].start()
+        else:
             tok_load.wait()
-        else:
-            sib_cp[0, 0].start()
         tok_cp[2, 2 * k].wait_recv()
         tok_cp[2, 2 * k + 1].wait_recv()
         gather(0, k)
         for q in (1, 2):
             x_cp[0, q, k].start()
     sib_cp[0, 1].start()
-    for k in range(2):
-        for pair in range(2):
-            x_cp[pair, 3, k].start()
 
     for pair in range(2):
         blocks = []
@@ -284,6 +293,13 @@
                 )
     hid_tile = 256
     for s in range(4):
+        if s == 1:
+            for k in range(2):
+                for pair in range(2):
+                    for q in (1, 2):
+                        x_cp[pair, q, k].wait_send()
+                for pair in range(2):
+                    x_cp[pair, 3, k].start()
         if s > 0:
             for part in range(2):
                 for k in range(2):
@@ -334,9 +350,11 @@
             lax.fori_loop(k * chunk // tile, (k + 1) * chunk // tile, down, 0)
             if s > 0:
                 for part in range(2):
+                    if s == 3 and k == 1:
+                        y_cp[s, part, 0].wait_send()
                     y_cp[s, part, k].start()
 
-    for cp in list(tok_cp.values()) + info_cp:
+    for cp in [tok_cp[2, q] for q in range(4)] + info_cp:
         cp.wait_send()
 
     def combine(pair, q):
@@ -417,7 +435,13 @@
         )
         store.start()
         stores.append(store)
-    for cp in [*x_cp.values(), *y_cp.values(), *part_cp.values(), *relay_cp]:
+    for pair in range(2):
+        for k in range(2):
+            x_cp[pair, 3, k].wait_send()
+    for (s, part, k), cp in y_cp.items():
+        if s < 3 or k == 1:
+            cp.wait_send()
+    for cp in [*part_cp.values(), *relay_cp]:
         cp.wait_send()
     for store in stores:
         store.wait()

time: 201 us -> 169 us (0.84)
  Pallas kernels: 195 us -> 163 us
    pallas_call x1, Pallas kernels: 195 us -> 163 us  [body(): pl.pallas_call(kernel, out_shape=jax.ShapeDtypeStruct((rows, half), BF16)...]
where the time goes in v3:
time: 169 us; the launch traced here: 168 us
  Pallas kernels  163 us (96%)
  local copies, waits for them, and re-layouts  4.98 us (3%)
    pallas_call x1, Pallas kernels, body(): pl.pallas_call(kernel, out_shape=jax.ShapeDtypeStruct((rows, half), BF16)...  163 us
    unnamed x3, local copies, waits for them, and re-layouts  4.98 us

profile of v3, /device:TPU:0, one launch (start us, length us, event | category | flops | bytes accessed | tf_op | source)
XLA Modules:
  0.0 168.3 jit_solution(5183212050862193559)
XLA Ops:
  0.0 1.4 copy.10.re_ref
  1.4 1.4 copy.11.rw_ref
  2.8 163.3 %routed_ffn.1 = bf16[128,3584]{1,0:T(8,128)(2,1)} custom-call(bf16[128,7168]{1,0:T(8,128)(2,1)} %tok_hbm.1, s32[128,8]{1,0:T(8,128)} %copy.10.re_ref, s32[128,8]{1,0:T(8,128)} %copy.11.rw_ref, bf16[1,7168,512]{2,1,0:T(8,128)(2,1)} %wg_hbm.1, bf16[1,7168,512]{2,1,0:T(8,128)(2,1)} %wu_hbm.1, bf16[1,512,7168]{2,1,0:T(8,128)(2,1)} %wd_hbm.1, f32[1,512]{1,0:T(1,128)} %sg_ref.1, ...), custom_call_target="tpu_custom_call" | custom-call | tf_op jit(solution)/shard_map/routed_ffn/pallas_call | solution.py:467
  166.1 2.2 %copy.13 = bf16[128,3584]{1,0:T(8,128)(2,1)} copy(bf16[128,3584]{1,0:T(8,128)(2,1)} %routed_ffn.1) | data formatting | bytes 1835008

commit v4 on v3

--- a/solution.py
+++ b/solution.py
@@ -146,23 +146,22 @@
     )
     wd_cp.start()
 
+    experts = SIDE * SIDE
     lane = lax.broadcasted_iota(jnp.int32, (TOK, TOK), 1)
     row = lax.broadcasted_iota(jnp.int32, (TOK, TOK), 0)
     wf = rw_ref[...].astype(F32)
-    mix = ROUTE_SCALE * wf / jnp.sum(wf, axis=1, keepdims=True)
-    chosen = jnp.zeros((TOK, TOK), F32)
-    weight = jnp.zeros((TOK, TOK), F32)
-    for k in range(re_ref.shape[1]):
-        hit = re_ref[:, k : k + 1] == lane
+    mix = ROUTE_SCALE * wf / jnp.sum(wf, axis=0, keepdims=True)
+    expert_row = lax.broadcasted_iota(jnp.int32, (experts, TOK), 0)
+    chosen = jnp.zeros((experts, TOK), F32)
+    weight = jnp.zeros((experts, TOK), F32)
+    for k in range(re_ref.shape[0]):
+        hit = re_ref[k : k + 1, :] == expert_row
         chosen = chosen + jnp.where(hit, 1.0, 0.0)
-        weight = weight + jnp.where(hit, mix[:, k : k + 1], 0.0)
-    chosen_t = chosen.T
-    weight_t = weight.T
+        weight = weight + jnp.where(hit, mix[k : k + 1, :], 0.0)
     before = jnp.where(row < lane, 1.0, 0.0).astype(BF16)
-    place_t = jnp.dot(chosen_t.astype(BF16), before, preferred_element_type=F32)
-    place_t = jnp.where(chosen_t > 0.5, place_t, -1.0)
-    info[0, 0:16] = place_t[0:16]
-    info[0, 16:32] = weight_t[0:16]
+    place = jnp.dot(chosen.astype(BF16), before, preferred_element_type=F32)
+    info[0, 0:experts] = jnp.where(chosen > 0.5, place, -1.0)
+    info[0, experts : 2 * experts] = weight
     info_cp = [
         remote(
             info.at[0],
@@ -282,13 +281,15 @@
     for s in range(1, 4):
         for part in range(2):
             pair = part_at(part, s)
-            for k in range(2):
-                away = pl.ds(pl.multiple_of((1 - c) * half + k * chunk, 128), chunk)
+            cuts = (0, chunk, half) if s < 3 else ends
+            for k in range(len(cuts) - 1):
+                size = cuts[k + 1] - cuts[k]
+                away = pl.ds(pl.multiple_of((1 - c) * half + cuts[k], 128), size)
                 y_cp[s, part, k] = remote(
                     x_buf.at[s, part * PAIR : (part + 1) * PAIR, away],
-                    ret.at[pair, s * PAIR : (s + 1) * PAIR, chunks[k]],
-                    y_s.at[2 * (2 * (s - 1) + part) + k],
-                    y_r.at[2 * (pair * 3 + s - 1) + k],
+                    ret.at[pair, s * PAIR : (s + 1) * PAIR, cuts[k] : cuts[k + 1]],
+                    y_s.at[4 * (2 * (s - 1) + part) + k],
+                    y_r.at[4 * (pair * 3 + s - 1) + k],
                     dev(part, back[s]),
                 )
     hid_tile = 256
@@ -300,11 +301,11 @@
                         x_cp[pair, q, k].wait_send()
                 for pair in range(2):
                     x_cp[pair, 3, k].start()
-        if s > 0:
+        for t in {1: (1, 2), 3: (3,)}.get(s, ()):
             for part in range(2):
                 for k in range(2):
-                    x_cp[part_at(part, s), s, k].wait_recv()
-                sib_cp[s, part].start()
+                    x_cp[part_at(part, t), t, k].wait_recv()
+                sib_cp[t, part].start()
         for part in range(2):
             sib_cp[s, part].wait()
         slot = s % 2
@@ -346,13 +347,20 @@
                 x_buf[s, :, at] = y
             return carry
 
-        for k in range(2):
-            lax.fori_loop(k * chunk // tile, (k + 1) * chunk // tile, down, 0)
-            if s > 0:
-                for part in range(2):
-                    if s == 3 and k == 1:
-                        y_cp[s, part, 0].wait_send()
-                    y_cp[s, part, k].start()
+        if s < 3:
+            for k in range(2):
+                lax.fori_loop(k * chunk // tile, (k + 1) * chunk // tile, down, 0)
+                if s > 0:
+                    for part in range(2):
+                        y_cp[s, part, k].start()
+        else:
+            lax.fori_loop(0, ends[1] // tile, down, 0)
+            for part in range(2):
+                y_cp[s, part, 0].start()
+            lax.fori_loop(ends[1] // tile, ends[2] // tile, down, 0)
+            for part in range(2):
+                y_cp[s, part, 1].start()
+            lax.fori_loop(ends[2] // tile, half // tile, down, 0)
 
     for cp in [tok_cp[2, q] for q in range(4)] + info_cp:
         cp.wait_send()
@@ -392,30 +400,36 @@
     ]
     part_cp = {}
     for i in range(2):
-        for k in range(2):
-            part_cp[i, k] = remote(
-                tok.at[1, i * TOK : (i + 1) * TOK, chunks[k]],
-                part_in.at[i, :, chunks[k]],
-                part_s.at[2 * i + k],
-                part_r.at[2 * i + k],
+        for q in range(4):
+            part_cp[i, q] = remote(
+                tok.at[1, i * TOK : (i + 1) * TOK, quarter[q]],
+                part_in.at[i, :, quarter[q]],
+                part_s.at[4 * i + q],
+                part_r.at[4 * i + q],
                 dev(1, (3, 1)[i]),
             )
 
-    def wait_rows(pair, k):
-        for q in range(1, 4):
-            y_cp[q, part_at(pair, q), k].wait_recv()
-
-    for k in range(2):
-        wait_rows(0, k)
-        for q in (2 * k, 2 * k + 1):
+    def wait_rows(pair, q):
+        if q % 2 == 0:
+            for s in (1, 2):
+                y_cp[s, part_at(pair, s), q // 2].wait_recv()
+        y_cp[3, part_at(pair, 3), q].wait_recv()
+
+    for q in range(5):
+        if q < 2:
+            for part in range(2):
+                y_cp[3, part, q].wait_send()
+                y_cp[3, part, q + 2].start()
+        if q < 4:
+            wait_rows(0, q)
             combine(0, q)
             relay_cp[q].start()
-        wait_rows(1, k)
-        for q in (2 * k, 2 * k + 1):
-            relay_cp[q].wait_recv()
-            combine(1, q)
-        for i in range(2):
-            part_cp[i, k].start()
+        if q > 0:
+            wait_rows(1, q - 1)
+            relay_cp[q - 1].wait_recv()
+            combine(1, q - 1)
+            for i in range(2):
+                part_cp[i, q - 1].start()
 
     def finish(n, carry):
         cols = pl.ds(pl.multiple_of(n * tile, tile), tile)
@@ -428,7 +442,8 @@
     stores = []
     for k in range(2):
         for i in range(2):
-            part_cp[i, k].wait_recv()
+            part_cp[i, 2 * k].wait_recv()
+            part_cp[i, 2 * k + 1].wait_recv()
         lax.fori_loop(k * chunk // tile, (k + 1) * chunk // tile, finish, 0)
         store = pltpu.make_async_copy(
             tok.at[0, 0:TOK, chunks[k]], out_hbm.at[:, chunks[k]], loc_sem.at[4 + k]
@@ -439,7 +454,7 @@
         for k in range(2):
             x_cp[pair, 3, k].wait_send()
     for (s, part, k), cp in y_cp.items():
-        if s < 3 or k == 1:
+        if s < 3 or k > 1:
             cp.wait_send()
     for cp in [*part_cp.values(), *relay_cp]:
         cp.wait_send()
@@ -496,10 +511,10 @@
             dma((8,)),
             dma((4,)),
             dma((4,)),
-            dma((12,)),
-            dma((12,)),
-            dma((4,)),
-            dma((4,)),
+            dma((24,)),
+            dma((24,)),
+            dma((8,)),
+            dma((8,)),
             dma((4,)),
             dma((4,)),
             dma((2,)),
@@ -510,8 +525,8 @@
         name="routed_ffn",
     )(
         tokens,
-        route_expert,
-        route_weight,
+        route_expert.T,
+        route_weight.T,
         gate_weight,
         up_weight,
         down_weight,

time: 169 us -> 159 us (0.941)
  Pallas kernels: 163 us -> 156 us
  local copies, waits for them, and re-layouts: 4.98 us -> 2.16 us
    pallas_call x1, Pallas kernels: 163 us -> 156 us  [body(): pl.pallas_call(kernel, out_shape=jax.ShapeDtypeStruct((rows, half), BF16)...]
    unnamed x3 -> x1, local copies, waits for them, and re-layouts: 4.98 us -> 2.16 us
where the time goes in v4:
time: 159 us; the launch traced here: 158 us
  Pallas kernels  156 us (98%)
  local copies, waits for them, and re-layouts  2.16 us (1%)
    pallas_call x1, Pallas kernels, body(): pl.pallas_call(kernel, out_shape=jax.ShapeDtypeStruct((rows, half), BF16)...  156 us

profile of v4, /device:TPU:0, one launch (start us, length us, event | category | flops | bytes accessed | tf_op | source)
XLA Modules:
  0.0 158.1 jit_solution(12059920928829161758)
XLA Ops:
  0.0 155.9 %routed_ffn.1 = bf16[128,3584]{1,0:T(8,128)(2,1)} custom-call(bf16[128,7168]{1,0:T(8,128)(2,1)} %tok_hbm.1, s32[8,128]{1,0:T(8,128)} %bitcast.2, s32[8,128]{1,0:T(8,128)} %bitcast.3, bf16[1,7168,512]{2,1,0:T(8,128)(2,1)} %wg_hbm.1, bf16[1,7168,512]{2,1,0:T(8,128)(2,1)} %wu_hbm.1, bf16[1,512,7168]{2,1,0:T(8,128)(2,1)} %wd_hbm.1, f32[1,512]{1,0:T(1,128)} %sg_ref.1, ...), custom_call_target="tpu_custom_call" | custom-call | tf_op jit(solution)/shard_map/routed_ffn/pallas_call | solution.py:482
  155.9 2.2 %copy.11 = bf16[128,3584]{1,0:T(8,128)(2,1)} copy(bf16[128,3584]{1,0:T(8,128)(2,1)} %routed_ffn.1) | data formatting | bytes 1835008

commit v5 on v4

--- a/solution.py
+++ b/solution.py
@@ -297,9 +297,6 @@
         if s == 1:
             for k in range(2):
                 for pair in range(2):
-                    for q in (1, 2):
-                        x_cp[pair, q, k].wait_send()
-                for pair in range(2):
                     x_cp[pair, 3, k].start()
         for t in {1: (1, 2), 3: (3,)}.get(s, ()):
             for part in range(2):
@@ -450,9 +447,8 @@
         )
         store.start()
         stores.append(store)
-    for pair in range(2):
-        for k in range(2):
-            x_cp[pair, 3, k].wait_send()
+    for cp in x_cp.values():
+        cp.wait_send()
     for (s, part, k), cp in y_cp.items():
         if s < 3 or k > 1:
             cp.wait_send()

time: 159 us -> 159 us (level)
  no operation moved by 1% of the time
where the time goes in v5:
time: 159 us; the launch traced here: 158 us
  Pallas kernels  156 us (98%)
  local copies, waits for them, and re-layouts  2.16 us (1%)
    pallas_call x1, Pallas kernels, body(): pl.pallas_call(kernel, out_shape=jax.ShapeDtypeStruct((rows, half), BF16)...  156 us

profile of v5, /device:TPU:0, one launch (start us, length us, event | category | flops | bytes accessed | tf_op | source)
XLA Modules:
  0.0 158.0 jit_solution(17488518416949363330)
XLA Ops:
  0.0 155.9 %routed_ffn.1 = bf16[128,3584]{1,0:T(8,128)(2,1)} custom-call(bf16[128,7168]{1,0:T(8,128)(2,1)} %tok_hbm.1, s32[8,128]{1,0:T(8,128)} %bitcast.2, s32[8,128]{1,0:T(8,128)} %bitcast.3, bf16[1,7168,512]{2,1,0:T(8,128)(2,1)} %wg_hbm.1, bf16[1,7168,512]{2,1,0:T(8,128)(2,1)} %wu_hbm.1, bf16[1,512,7168]{2,1,0:T(8,128)(2,1)} %wd_hbm.1, f32[1,512]{1,0:T(1,128)} %sg_ref.1, ...), custom_call_target="tpu_custom_call" | custom-call | tf_op jit(solution)/shard_map/routed_ffn/pallas_call | solution.py:478
  155.9 2.2 %copy.11 = bf16[128,3584]{1,0:T(8,128)(2,1)} copy(bf16[128,3584]{1,0:T(8,128)(2,1)} %routed_ffn.1) | data formatting | bytes 1835008
